TPU v7x, 32 devices: a whole 2x2x4 slice. The times are simulated.
32 devices in a mesh: grp: 2 (over x), row: 8 (over z, y), col: 2 (over core).
Axes of the slice: x: 2, y: 2, z: 4, core: 2. Of those that a mesh axis runs over, the one named last changes fastest.
Arguments:
- three_centre: bfloat16 [128, 1024, 1024], P(None, ('row', 'col')), may hold values from -6 to 6
- green_occ: bfloat16 [2048, 1024], P(('grp', 'row', 'col')), parts along dimension 0, may hold values from -0.25 to 0.25
- green_virt: bfloat16 [2048, 1024], P(('grp', 'row', 'col')), parts along dimension 0, may hold values from -0.25 to 0.25
- mask_three: int32 [1, 8, 8], replicated, may hold values 0 or 1
- mask_occ: int32 [16, 8], P('grp'), parts along dimension 0, may hold values 0 or 1
- mask_virt: int32 [16, 8], P('grp'), parts along dimension 0, may hold values 0 or 1
Outputs:
- half_done: bfloat16 [256, 1024, 1024], P('grp', ('row', 'col')), parts along dimension 0
- response: float32 [256, 128], P('grp'), parts along dimension 0
There are 2 independent parts, one for each index of `grp`. A program takes and returns all parts, laid end to end along the dimension named above; an argument that names none is the same for every part. Nothing has to cross between parts.
All inputs are finite; a program needn't handle non-finite values.
Results may differ from a plain program's by a relative error of at most 0.0053.
Values may be sent and summed in bfloat16 or wider, within the bound.
A program may use at most 192 MiB of HBM per device.

v0:
```python
import jax
import jax.numpy as jnp
from jax import lax
from jax.sharding import PartitionSpec as P


def expand_rows(small_mask, first_row, row_count, block_size):
    tall = jnp.repeat(small_mask, block_size, axis=0)
    tall = lax.dynamic_slice_in_dim(tall, first_row, row_count, 0)
    return jnp.repeat(tall, block_size, axis=1)


def local(three_centre, green_occ, green_virt, mask_three, mask_occ, mask_virt):
    dev_index = lax.axis_index(("row", "col"))
    ri_count, local_rows, ao_count = three_centre.shape
    block_count = mask_occ.shape[0]
    block_size = ao_count // block_count
    ri_blocks = mask_three.shape[0]
    first_row = dev_index * local_rows
    occ_local = green_occ * expand_rows(mask_occ, first_row, local_rows, block_size).astype(
        jnp.bfloat16
    )
    virt_local = green_virt * expand_rows(mask_virt, first_row, local_rows, block_size).astype(
        jnp.bfloat16
    )
    three_mask = lax.dynamic_slice_in_dim(
        jnp.repeat(mask_three, block_size, axis=1), first_row, local_rows, 1
    )
    masked = (
        three_centre.reshape(ri_blocks, block_size, local_rows, block_count, block_size)
        * three_mask[:, None, :, :, None].astype(jnp.bfloat16)
    ).reshape(ri_count, local_rows, ao_count)
    masked_rows = masked.reshape(ri_count * local_rows, ao_count)
    occ_full, virt_full = (
        lax.all_gather(occ_local, ("row", "col"), axis=0, tiled=True),
        lax.all_gather(virt_local, ("row", "col"), axis=0, tiled=True),
    )
    first_sum = jnp.dot(masked_rows, occ_full, preferred_element_type=jnp.float32)
    transformed = first_sum.astype(jnp.bfloat16).reshape(ri_count, local_rows, ao_count)
    arrived = lax.all_to_all(transformed, ("row", "col"), split_axis=2, concat_axis=1, tiled=True)
    swapped = jnp.swapaxes(arrived, 1, 2)
    swapped_rows = swapped.reshape(ri_count * local_rows, ao_count)
    second_sum = jnp.dot(swapped_rows, virt_full, preferred_element_type=jnp.float32)
    xform = second_sum.astype(jnp.bfloat16).reshape(ri_count, local_rows * ao_count)
    partial_value = lax.dot_general(
        xform,
        masked.reshape(ri_count, local_rows * ao_count),
        (((1,), (1,)), ((), ())),
        preferred_element_type=jnp.float32,
    )
    summed = lax.psum(partial_value, ("row", "col"))
    response = -summed / ao_count
    return (swapped, response)


def solution(mesh):
    in_specs = (
        P(None, ("row", "col"), None),
        P(("grp", "row", "col"), None),
        P(("grp", "row", "col"), None),
        P(),
        P("grp", None),
        P("grp", None),
    )
    out_specs = (P("grp", ("row", "col"), None), P("grp", None))
    return jax.shard_map(local, mesh=mesh, in_specs=in_specs, out_specs=out_specs, check_vma=False)
```

profile of v0, /device:TPU:0, one launch (start us, length us, event | category | flops | bytes accessed | tf_op | source)
XLA Modules:
  0.0 686.8 jit_solution(4759023042982545078)
XLA Ops:
  7.2 0.0 all-gather.3.cloned.1.call-start
  7.2 0.7 broadcast_in_dim.20
  7.9 0.7 broadcast_in_dim.22
  8.7 0.1 broadcast_in_dim.21
  8.8 1.6 bitcast_multiply_fusion.5
  10.4 0.0 all-gather.3.cloned.1.call-update
  10.4 0.7 broadcast_in_dim.18
  11.2 43.7 %all-gather.3.cloned.1.call-done = bf16[1024,1024]{1,0:T(8,128)(2,1)} async-done(((bf16[64,1024]{1,0:T(8,128)(2,1)}), bf16[1024,1024]{1,0:T(8,128)(2,1)}) %all-gather.3.cloned.1.call-update) | async-done | bytes 2097168 | tf_op jit(solution)/shard_map/all_gather | solution.py:35
  54.9 0.0 copy-start.1
  54.9 6.5 mul.39
  61.3 0.0 copy-done.1
  61.3 24.9 %fusion.2 = bf16[8192,1024]{1,0:T(8,128)(2,1)} fusion(bf16[1024,1024]{1,0:T(8,128)(2,1)S(1)} %copy-done.1, bf16[8192,1024]{1,0:T(8,128)(2,1)} %bitcast.41, bf16[1024,8,8,128]{3,2,1,0:T(8,128)(2,1)} %bitcast.40), kind=kOutput, calls=%fused_computation.3 | convolution fusion | flops 17196646400 | bytes 52428800 | tf_op jit(solution)/shard_map/dot_general | solution.py:38
  86.3 25.9 %copy.16 = bf16[128,64,1024]{0,1,2:T(8,128)(2,1)} copy(bf16[128,64,1024]{2,1,0:T(8,128)(2,1)} %bitcast.43) | data formatting | bytes 33554432 | tf_op jit(solution)/shard_map/reshape | solution.py:39
  112.2 5.3 all-to-all-start
  117.5 0.0 all-gather.5.cloned.1.call-start
  117.5 0.1 broadcast_in_dim.23
  117.7 0.0 copy-done
  117.7 0.7 bitcast_multiply_fusion.4
  118.4 0.0 all-gather.5.cloned.1.call-update
  118.4 0.2 all-reduce.2.cloned.1.call-start
  118.6 0.1 mul.44
  118.8 8.0 %broadcast_multiply_fusion = bf16[128,64,1024]{2,1,0:T(8,128)(2,1)S(1)} fusion(bf16[128,64,1024]{2,1,0:T(8,128)(2,1)} %param.6, bf16[64,1024]{1,0:T(8,128)(2,1)S(1)} %bitcast.47), kind=kLoop, calls=%fused_computation.5 | loop fusion | flops 8388608 | bytes 33685504 | tf_op jit(solution)/shard_map/mul | solution.py:30
  126.8 11.1 %copy.26 = bf16[16,8,64,1024]{3,1,2,0:T(8,128)(2,1)} copy(bf16[16,8,64,1024]{3,2,1,0:T(8,128)(2,1)S(1)} %bitcast.38) | data formatting | bytes 33554432
  137.9 288.9 %all-to-all-done = bf16[128,64,1024]{0,1,2:T(8,128)(2,1)} async-done(((bf16[128,64,1024]{0,1,2:T(8,128)(2,1)}), bf16[128,64,1024]{0,1,2:T(8,128)(2,1)}, u32[]{:S(2)}, u32[]{:S(2)}) %all-to-all-start) | async-done | bytes 16777248 | tf_op jit(solution)/shard_map/all_to_all | solution.py:40
  426.8 18.5 %copy.18 = bf16[128,16,64,64]{0,3,2,1:T(8,128)(2,1)} copy(bf16[128,16,64,64]{0,2,3,1:T(8,128)(2,1)} %bitcast.7) | data formatting | bytes 33554432 | tf_op jit(solution)/shard_map/all_to_all | solution.py:40
  445.3 25.9 %copy.20 = bf16[128,64,1024]{2,1,0:T(8,128)(2,1)} copy(bf16[128,64,1024]{0,1,2:T(8,128)(2,1)} %bitcast.39) | data formatting | bytes 33554432
  471.3 23.6 %convolution_convert_fusion = bf16[8192,1024]{1,0:T(8,128)(2,1)} fusion(bf16[8192,1024]{1,0:T(8,128)(2,1)} %bitcast.42, bf16[1024,1024]{1,0:T(8,128)(2,1)} %all-gather.5.cloned.1.call-done), kind=kOutput, calls=%fused_computation.4 | convolution fusion | flops 17188257792 | bytes 35651584 | tf_op jit(solution)/shard_map/dot_general | solution.py:43
  494.9 20.4 %reshape.57 = bf16[128,65536]{1,0:T(8,128)(2,1)} reshape(bf16[8192,1024]{1,0:T(8,128)(2,1)} %convolution_convert_fusion) | data formatting | bytes 33554432 | tf_op jit(solution)/shard_map/reshape | solution.py:44
  515.3 13.5 %fusion.3 = f32[128,128]{1,0:T(8,128)} fusion(bf16[128,65536]{1,0:T(8,128)(2,1)} %reshape.57, bf16[128,65536]{1,0:T(8,128)(2,1)} %bitcast.37), kind=kOutput, calls=%fused_computation.13 | convolution fusion | flops 2147483648 | bytes 33619968 | tf_op jit(solution)/shard_map/dot_general | solution.py:45
  528.8 0.0 all-reduce.2.cloned.1.call-update
  528.8 150.0 %all-reduce.2.cloned.1.call-done = f32[128,128]{1,0:T(8,128)} async-done(((f32[128,128]{1,0:T(8,128)}), f32[128,128]{1,0:T(8,128)}) %all-reduce.2.cloned.1.call-update) | async-done | bytes 65552 | tf_op jit(solution)/shard_map/psum | solution.py:51
  678.8 1.5 negate_multiply_fusion
  (5 shorter events, 0.1 us)
Async XLA Ops:
  7.2 47.7 %all-gather.3.cloned.1.call-start = ((), (), s32[]{:S(2)}) async-start(), calls=%async_computation.1 | async-start | bytes 2228224 | tf_op jit(solution)/shard_map/all_gather | solution.py:35
  54.9 6.5 copy-start.1
  112.2 5.5 copy-start
  112.2 314.6 %all-to-all-start = ((bf16[128,64,1024]{0,1,2:T(8,128)(2,1)}), bf16[128,64,1024]{0,1,2:T(8,128)(2,1)}, u32[]{:S(2)}, u32[]{:S(2)}) async-start(bf16[128,64,1024]{0,1,2:T(8,128)(2,1)} %copy.16), calls=%async_computation | async-start | bytes 33554432 | tf_op jit(solution)/shard_map/all_to_all | solution.py:40
  117.5 353.8 %all-gather.5.cloned.1.call-start = ((), (), s32[]{:S(2)}) async-start(), calls=%async_computation.2 | async-start | bytes 2228224 | tf_op jit(solution)/shard_map/all_gather | solution.py:36
  118.4 560.5 %all-reduce.2.cloned.1.call-start = ((), (), s32[]{:S(2)}) async-start(), calls=%async_computation.3 | async-start | bytes 131072 | tf_op jit(solution)/shard_map/psum | solution.py:51
Sparse Core Ops, SparseCore 0:
  10.7 44.0 all-gather.2
  120.5 241.4 all-gather.4
  529.0 149.8 all-reduce.1
where the time goes:
time: 690 us; the launch traced here: 687 us
  waiting for transfers between devices  483 us (70%)
  local copies, waits for them, and re-layouts  111 us (16%)
  matrix products  62.1 us (9%)
  between operations  13.8 us (2%)
  other arithmetic  11.7 us (2%)
    all_to_all x1, waiting for transfers between devices, local(): lax.all_to_all(transformed, ('row', 'col'), split_axis=2, concat_axis=1,...  289 us
    psum x1, waiting for transfers between devices, local(): summed = lax.psum(partial_value, ('row', 'col'))  150 us
    all_gather x1, waiting for transfers between devices, local(): lax.all_gather(occ_local, ('row', 'col'), axis=0, tiled=True)  43.7 us
    unnamed x7, local copies, waits for them, and re-layouts  37.1 us
    reshape x1, local copies, waits for them, and re-layouts, local(): first_sum.astype(jnp.bfloat16).reshape(ri_count, local_rows, ao_count)  25.9 us
    dot_general x1, matrix products, local(): jnp.dot(masked_rows, occ_full, preferred_element_type=jnp.float32)  24.9 us
    dot_general x1, matrix products, local(): jnp.dot(swapped_rows, virt_full, preferred_element_type=jnp.float32)  23.6 us
    reshape x1, local copies, waits for them, and re-layouts, local(): second_sum.astype(jnp.bfloat16).reshape(ri_count, local_rows * ao_count)  20.4 us
  transfers between devices with their start and end apart: 4, of which 3 were waited for; matrix products, arithmetic and copies ran while one was open for 9% of the time, Pallas kernels for 0%

commit v1 on v0

--- a/solution.py
+++ b/solution.py
@@ -1,7 +1,16 @@
+import functools
+
 import jax
 import jax.numpy as jnp
 from jax import lax
+from jax.experimental import pallas as pl
+from jax.experimental.pallas import tpu as pltpu
 from jax.sharding import PartitionSpec as P
+
+AXES = ("row", "col")
+CHUNKS = 4
+STEP = 8
+VMEM = 48 * 2**20
 
 
 def expand_rows(small_mask, first_row, row_count, block_size):
@@ -10,7 +19,7 @@
     return jnp.repeat(tall, block_size, axis=1)
 
 
-def local(three_centre, green_occ, green_virt, mask_three, mask_occ, mask_virt):
+def local_plain(three_centre, green_occ, green_virt, mask_three, mask_occ, mask_virt):
     dev_index = lax.axis_index(("row", "col"))
     ri_count, local_rows, ao_count = three_centre.shape
     block_count = mask_occ.shape[0]
@@ -53,7 +62,161 @@
     return (swapped, response)
 
 
+def first_kernel(weight_ref, rows_ref, sent_ref):
+    step, rows, depth = rows_ref.shape
+    flat = rows_ref[...].reshape(step * rows, depth)
+    product = lax.dot_general(
+        weight_ref[...], flat, (((1,), (1,)), ((), ())), preferred_element_type=jnp.float32
+    ).astype(jnp.bfloat16)
+    owners, pairs, width, lanes = sent_ref.shape
+    for pair in range(pairs):
+        sent_ref[:, pair] = product[:, pair * lanes : (pair + 1) * lanes].reshape(
+            owners, width, lanes
+        )
+
+
+def second_kernel(came_ref, weight_ref, *refs):
+    half_ref, xform_ref = refs[-2:]
+    owners, pairs, width, lanes = came_ref.shape
+    for pair in range(pairs):
+        for tile in range(owners // 2):
+            even, odd = came_ref[2 * tile, pair], came_ref[2 * tile + 1, pair]
+            spot = slice(tile * lanes, (tile + 1) * lanes)
+            half_ref[2 * pair, :, spot] = jnp.concatenate(
+                [even[:, :width], odd[:, :width]], axis=-1
+            )
+            half_ref[2 * pair + 1, :, spot] = jnp.concatenate(
+                [even[:, width:], odd[:, width:]], axis=-1
+            )
+    step, rows, depth = half_ref.shape
+    product = jnp.dot(
+        half_ref[...].reshape(step * rows, depth),
+        weight_ref[...],
+        preferred_element_type=jnp.float32,
+    )
+    xform_ref[...] = product.astype(jnp.bfloat16).reshape(step, rows, depth)
+
+
+def transform_chunk(weight, three_centre, chunk, chunk_size, owners):
+    ri_count, rows, depth = three_centre.shape
+    steps = chunk_size // STEP
+    return pl.pallas_call(
+        first_kernel,
+        grid=(steps,),
+        in_specs=[
+            pl.BlockSpec((depth, depth), lambda i: (0, 0)),
+            pl.BlockSpec((STEP, rows, depth), lambda i: (chunk * steps + i, 0, 0)),
+        ],
+        out_specs=pl.BlockSpec((owners, STEP // 2, rows, 2 * rows), lambda i: (0, i, 0, 0)),
+        out_shape=jax.ShapeDtypeStruct((owners, chunk_size // 2, rows, 2 * rows), jnp.bfloat16),
+        compiler_params=pltpu.CompilerParams(vmem_limit_bytes=VMEM),
+        cost_estimate=pl.CostEstimate(
+            flops=2 * chunk_size * rows * depth * depth,
+            bytes_accessed=4 * chunk_size * rows * depth + 2 * depth * depth,
+            transcendentals=0,
+        ),
+    )(weight, three_centre)
+
+
+def finish_chunk(came, weight, half, chunk, chunk_size, ri_count):
+    owners, pairs, rows, lanes = came.shape
+    depth = weight.shape[0]
+    steps = chunk_size // STEP
+    operands = [came, weight]
+    in_specs = [
+        pl.BlockSpec((owners, STEP // 2, rows, lanes), lambda i: (0, i, 0, 0)),
+        pl.BlockSpec((depth, depth), lambda i: (0, 0)),
+    ]
+    aliases = {}
+    if half is not None:
+        operands.append(half)
+        in_specs.append(pl.BlockSpec(memory_space=pl.ANY))
+        aliases = {2: 0}
+    return pl.pallas_call(
+        second_kernel,
+        grid=(steps,),
+        in_specs=in_specs,
+        out_specs=[
+            pl.BlockSpec((STEP, rows, depth), lambda i: (chunk * steps + i, 0, 0)),
+            pl.BlockSpec((STEP, rows, depth), lambda i: (i, 0, 0)),
+        ],
+        out_shape=[
+            jax.ShapeDtypeStruct((ri_count, rows, depth), jnp.bfloat16),
+            jax.ShapeDtypeStruct((chunk_size, rows, depth), jnp.bfloat16),
+        ],
+        input_output_aliases=aliases,
+        compiler_params=pltpu.CompilerParams(vmem_limit_bytes=VMEM),
+        cost_estimate=pl.CostEstimate(
+            flops=2 * chunk_size * rows * depth * depth,
+            bytes_accessed=6 * chunk_size * rows * depth + 2 * depth * depth,
+            transcendentals=0,
+        ),
+    )(*operands)
+
+
+def spread(mask, block_size):
+    return jnp.repeat(jnp.repeat(mask, block_size, 0), block_size, 1).astype(jnp.bfloat16)
+
+
+def sum_over_devices(value, owners):
+    pieces = value.reshape(owners, value.shape[0] // owners, value.shape[1])
+    pieces = lax.all_to_all(pieces, AXES, split_axis=0, concat_axis=0, tiled=True)
+    total = jnp.sum(pieces, axis=0)
+    copies = jnp.broadcast_to(total[None], pieces.shape)
+    copies = lax.all_to_all(copies, AXES, split_axis=0, concat_axis=0, tiled=True)
+    return copies.reshape(value.shape)
+
+
+def local_fused(owners, three_centre, green_occ, green_virt, mask_three, mask_occ, mask_virt):
+    ri_count, rows, depth = three_centre.shape
+    block_size = depth // mask_occ.shape[0]
+    chunk_size = ri_count // CHUNKS
+    own_block = lax.axis_index(AXES) * rows // block_size
+    own_mask = lax.dynamic_slice_in_dim(mask_three[0], own_block, 1, 0)
+    occ_full = lax.all_gather(green_occ, AXES, axis=0, tiled=True)
+    virt_full = lax.all_gather(green_virt, AXES, axis=0, tiled=True)
+    occ_weight = occ_full.T * spread(mask_occ.T * own_mask, block_size)
+    virt_weight = virt_full * spread(mask_virt * own_mask, block_size)
+    sent = [
+        transform_chunk(occ_weight, three_centre, chunk, chunk_size, owners)
+        for chunk in range(CHUNKS)
+    ]
+    came = [
+        lax.all_to_all(block, AXES, split_axis=0, concat_axis=0, tiled=True) for block in sent
+    ]
+    half, parts = None, []
+    for chunk in range(CHUNKS):
+        half, xform = finish_chunk(came[chunk], virt_weight, half, chunk, chunk_size, ri_count)
+        parts.append(
+            lax.dot_general(
+                xform,
+                three_centre,
+                (((1, 2), (1, 2)), ((), ())),
+                preferred_element_type=jnp.float32,
+            )
+        )
+    response = -sum_over_devices(jnp.concatenate(parts, axis=0), owners) / depth
+    return half, response
+
+
+def local(owners, three_centre, green_occ, green_virt, mask_three, mask_occ, mask_virt):
+    ri_count, rows, depth = three_centre.shape
+    block_size = depth // mask_occ.shape[0]
+    fits = (
+        mask_three.shape[0] == 1
+        and 2 * rows == 128
+        and block_size % rows == 0
+        and owners % 2 == 0
+        and owners * rows == depth
+        and ri_count % (CHUNKS * STEP) == 0
+        and ri_count % owners == 0
+    )
+    body = functools.partial(local_fused, owners) if fits else local_plain
+    return body(three_centre, green_occ, green_virt, mask_three, mask_occ, mask_virt)
+
+
 def solution(mesh):
+    owners = mesh.shape["row"] * mesh.shape["col"]
     in_specs = (
         P(None, ("row", "col"), None),
         P(("grp", "row", "col"), None),
@@ -63,4 +226,5 @@
         P("grp", None),
     )
     out_specs = (P("grp", ("row", "col"), None), P("grp", None))
-    return jax.shard_map(local, mesh=mesh, in_specs=in_specs, out_specs=out_specs, check_vma=False)
+    return jax.shard_map(
+        functools.partial(local, owners), mesh=mesh, in_specs=in_specs, out_specs=out_specs, check_vma=False)

time: 690 us -> 645 us (0.935)
  waiting for transfers between devices: 483 us -> 340 us
  local copies, waits for them, and re-layouts: 111 us -> 10 us
  Pallas kernels: 0 us -> 64 us
  starting transfers between devices: 5.58 us -> 64 us
  matrix products: 62.1 us -> 117 us
  blocking collectives: 0 us -> 23.9 us
    psum x1 -> x0, waiting for transfers between devices: 150 us -> none  [local(): summed = lax.psum(partial_value, ('row', 'col'))]
    all_gather x2, waiting for transfers between devices: 43.7 us -> 130 us  [the longest x1 84.3 us: local_fused(): virt_full = lax.all_gather(green_virt, AXES, axis=0, tiled=True)]
    all_to_all x1 -> x4, waiting for transfers between devices: 289 us -> 210 us  [local_fused(): lax.all_to_all(block, AXES, split_axis=0, concat_axis=0, tiled=True)]
    pallas_call x0 -> x8, Pallas kernels: none -> 64 us  [the longest x4 32.8 us: finish_chunk(): pl.pallas_call(second_kernel, grid=(steps,), in_specs=in_specs, out_specs...]
    all_to_all x1 -> x4, starting transfers between devices: 5.28 us -> 63.6 us  [local_fused(): lax.all_to_all(block, AXES, split_axis=0, concat_axis=0, tiled=True)]
    dot_general x3 -> x4, matrix products: 62.1 us -> 117 us  [local_fused(): lax.dot_general(xform, three_centre, (((1, 2), (1, 2)), ((), ())), prefer...]
    reshape x2 -> x0, local copies, waits for them, and re-layouts: 46.4 us -> none  [the longest x1 25.9 us: local(): first_sum.astype(jnp.bfloat16).reshape(ri_count, local_rows, ao_count)]
    unnamed x7 -> x4, local copies, waits for them, and re-layouts: 37.1 us -> 0.02 us
  transfers between devices with their start and end apart: 4 -> 6, of which waited for: 3 -> 5; matrix products, arithmetic and copies ran while one was open for 9% -> 1% of each run, Pallas kernels for 0% -> 7%
where the time goes in v1:
time: 645 us; the launch traced here: 638 us
  waiting for transfers between devices  340 us (53%)
  matrix products  117 us (18%)
  starting transfers between devices  64 us (10%)
  Pallas kernels  64 us (10%)
  blocking collectives  23.9 us (4%)
  between operations  14.4 us (2%)
  local copies, waits for them, and re-layouts  10 us (2%)
    all_to_all x4, waiting for transfers between devices, local_fused(): lax.all_to_all(block, AXES, split_axis=0, concat_axis=0, tiled=True)  210 us
    dot_general x4, matrix products, local_fused(): lax.dot_general(xform, three_centre, (((1, 2), (1, 2)), ((), ())), prefer...  117 us
    all_gather x1, waiting for transfers between devices, local_fused(): virt_full = lax.all_gather(green_virt, AXES, axis=0, tiled=True)  84.3 us
    all_to_all x4, starting transfers between devices, local_fused(): lax.all_to_all(block, AXES, split_axis=0, concat_axis=0, tiled=True)  63.6 us
    all_gather x1, waiting for transfers between devices, local_fused(): occ_full = lax.all_gather(green_occ, AXES, axis=0, tiled=True)  45.5 us
    pallas_call x4, Pallas kernels, finish_chunk(): pl.pallas_call(second_kernel, grid=(steps,), in_specs=in_specs, out_specs...  32.8 us
    pallas_call x4, Pallas kernels, transform_chunk(): pl.pallas_call(first_kernel, grid=(steps,), in_specs=[pl.BlockSpec((depth...  31.2 us
    all_to_all x1, blocking collectives, sum_over_devices(): lax.all_to_all(pieces, AXES, split_axis=0, concat_axis=0, tiled=True)  14.4 us
  transfers between devices with their start and end apart: 6, of which 5 were waited for; matrix products, arithmetic and copies ran while one was open for 1% of the time, Pallas kernels for 7%

profile of v1, /device:TPU:0, one launch (start us, length us, event | category | flops | bytes accessed | tf_op | source)
XLA Modules:
  0.0 638.5 jit_solution(13588162066361304245)
XLA Ops:
  7.2 0.7 all-gather.3.cloned.1.call-update
  8.0 0.8 multiply_convert_fusion
  8.8 45.5 %all-gather.3.cloned.1.call-done = bf16[1024,1024]{1,0:T(8,128)(2,1)} async-done(((bf16[64,1024]{1,0:T(8,128)(2,1)}), bf16[1024,1024]{1,0:T(8,128)(2,1)}) %all-gather.3.cloned.1.call-update) | async-done | bytes 2097168 | tf_op jit(solution)/shard_map/all_gather | solution.py:176
  54.3 3.9 copy.21
  58.3 2.9 broadcast_in_dim.19
  61.2 1.9 bitcast_multiply_fusion.1.weight_ref
  63.1 7.8 %shard_map.80 = bf16[16,16,64,128]{3,2,1,0:T(8,128)(2,1)} custom-call(bf16[1024,1024]{1,0:T(8,128)(2,1)S(1)} %bitcast_multiply_fusion.1.weight_ref, bf16[128,64,1024]{2,1,0:T(8,128)(2,1)} %rows_ref.7), custom_call_target="tpu_custom_call" | custom-call | flops 4294967296 | bytes 10485760 | tf_op jit(solution)/shard_map/pallas_call | solution.py:103
  70.9 4.5 all-to-all-start.3
  75.4 7.8 %shard_map.79 = bf16[16,16,64,128]{3,2,1,0:T(8,128)(2,1)} custom-call(bf16[1024,1024]{1,0:T(8,128)(2,1)S(1)} %bitcast_multiply_fusion.1.weight_ref, bf16[128,64,1024]{2,1,0:T(8,128)(2,1)} %rows_ref.7), custom_call_target="tpu_custom_call" | custom-call | flops 4294967296 | bytes 10485760 | tf_op jit(solution)/shard_map/pallas_call | solution.py:103
  83.3 69.8 %all-to-all-done.3.came_ref = bf16[16,16,64,128]{3,2,1,0:T(8,128)(2,1)} async-done(((bf16[16,16,64,128]{3,2,1,0:T(8,128)(2,1)}), bf16[16,16,64,128]{3,2,1,0:T(8,128)(2,1)}, u32[]{:S(2)}, u32[]{:S(2)}) %all-to-all-start.3) | async-done | bytes 4194336 | tf_op jit(solution)/shard_map/all_to_all | solution.py:185
  153.0 19.7 %all-to-all-start.2 = ((bf16[16,16,64,128]{3,2,1,0:T(8,128)(2,1)}), bf16[16,16,64,128]{3,2,1,0:T(8,128)(2,1)}, u32[]{:S(2)}, u32[]{:S(2)}) async-start(bf16[16,16,64,128]{3,2,1,0:T(8,128)(2,1)} %shard_map.79), calls=%async_computation.2 | async-start | bytes 8388608 | tf_op jit(solution)/shard_map/all_to_all | solution.py:185
  172.7 7.8 %shard_map.78 = bf16[16,16,64,128]{3,2,1,0:T(8,128)(2,1)} custom-call(bf16[1024,1024]{1,0:T(8,128)(2,1)S(1)} %bitcast_multiply_fusion.1.weight_ref, bf16[128,64,1024]{2,1,0:T(8,128)(2,1)} %rows_ref.7), custom_call_target="tpu_custom_call" | custom-call | flops 4294967296 | bytes 10485760 | tf_op jit(solution)/shard_map/pallas_call | solution.py:103
  180.5 69.9 %all-to-all-done.2.came_ref = bf16[16,16,64,128]{3,2,1,0:T(8,128)(2,1)} async-done(((bf16[16,16,64,128]{3,2,1,0:T(8,128)(2,1)}), bf16[16,16,64,128]{3,2,1,0:T(8,128)(2,1)}, u32[]{:S(2)}, u32[]{:S(2)}) %all-to-all-start.2) | async-done | bytes 4194336 | tf_op jit(solution)/shard_map/all_to_all | solution.py:185
  250.4 19.7 %all-to-all-start.1 = ((bf16[16,16,64,128]{3,2,1,0:T(8,128)(2,1)}), bf16[16,16,64,128]{3,2,1,0:T(8,128)(2,1)}, u32[]{:S(2)}, u32[]{:S(2)}) async-start(bf16[16,16,64,128]{3,2,1,0:T(8,128)(2,1)} %shard_map.78), calls=%async_computation.1 | async-start | bytes 8388608 | tf_op jit(solution)/shard_map/all_to_all | solution.py:185
  270.1 7.8 %shard_map.77 = bf16[16,16,64,128]{3,2,1,0:T(8,128)(2,1)} custom-call(bf16[1024,1024]{1,0:T(8,128)(2,1)S(1)} %bitcast_multiply_fusion.1.weight_ref, bf16[128,64,1024]{2,1,0:T(8,128)(2,1)} %rows_ref.7), custom_call_target="tpu_custom_call" | custom-call | flops 4294967296 | bytes 10485760 | tf_op jit(solution)/shard_map/pallas_call | solution.py:103
  277.9 69.9 %all-to-all-done.1.came_ref = bf16[16,16,64,128]{3,2,1,0:T(8,128)(2,1)} async-done(((bf16[16,16,64,128]{3,2,1,0:T(8,128)(2,1)}), bf16[16,16,64,128]{3,2,1,0:T(8,128)(2,1)}, u32[]{:S(2)}, u32[]{:S(2)}) %all-to-all-start.1) | async-done | bytes 4194336 | tf_op jit(solution)/shard_map/all_to_all | solution.py:185
  347.8 19.7 %all-to-all-start = ((bf16[16,16,64,128]{3,2,1,0:T(8,128)(2,1)}), bf16[16,16,64,128]{3,2,1,0:T(8,128)(2,1)}, u32[]{:S(2)}, u32[]{:S(2)}) async-start(bf16[16,16,64,128]{3,2,1,0:T(8,128)(2,1)} %shard_map.77), calls=%async_computation | async-start | bytes 8388608 | tf_op jit(solution)/shard_map/all_to_all | solution.py:185
  367.8 0.4 all-gather.5.cloned.1.call-update
  368.2 84.3 %all-gather.5.cloned.1.call-done = bf16[1024,1024]{1,0:T(8,128)(2,1)} async-done(((bf16[64,1024]{1,0:T(8,128)(2,1)}), bf16[1024,1024]{1,0:T(8,128)(2,1)}) %all-gather.5.cloned.1.call-update) | async-done | bytes 2097168 | tf_op jit(solution)/shard_map/all_gather | solution.py:177
  452.6 2.9 broadcast_in_dim.21
  455.5 1.9 bitcast_multiply_fusion.weight_ref
  457.4 8.1 %shard_map.81 = (bf16[128,64,1024]{2,1,0:T(8,128)(2,1)}, bf16[32,64,1024]{2,1,0:T(8,128)(2,1)}) custom-call(bf16[16,16,64,128]{3,2,1,0:T(8,128)(2,1)} %all-to-all-done.3.came_ref, bf16[1024,1024]{1,0:T(8,128)(2,1)S(1)} %bitcast_multiply_fusion.weight_ref), custom_call_target="tpu_custom_call" | custom-call | flops 4294967296 | bytes 14680064 | tf_op jit(solution)/shard_map/pallas_call | solution.py:135
  465.5 8.1 %shard_map.82 = (bf16[128,64,1024]{2,1,0:T(8,128)(2,1)}, bf16[32,64,1024]{2,1,0:T(8,128)(2,1)}) custom-call(bf16[16,16,64,128]{3,2,1,0:T(8,128)(2,1)} %all-to-all-done.2.came_ref, bf16[1024,1024]{1,0:T(8,128)(2,1)S(1)} %bitcast_multiply_fusion.weight_ref, bf16[128,64,1024]{2,1,0:T(8,128)(2,1)} %get-tuple-element.10.refs_0_), custom_call_target="tpu_custom_call", output_to_operand_aliasing={{0}: (2, {})} | custom-call | flops 4294967296 | bytes 14680064 | tf_op jit(solution)/shard_map/pallas_call | solution.py:135
  473.6 8.1 %shard_map.83 = (bf16[128,64,1024]{2,1,0:T(8,128)(2,1)}, bf16[32,64,1024]{2,1,0:T(8,128)(2,1)}) custom-call(bf16[16,16,64,128]{3,2,1,0:T(8,128)(2,1)} %all-to-all-done.1.came_ref, bf16[1024,1024]{1,0:T(8,128)(2,1)S(1)} %bitcast_multiply_fusion.weight_ref, bf16[128,64,1024]{2,1,0:T(8,128)(2,1)} %get-tuple-element.11.refs_0_), custom_call_target="tpu_custom_call", output_to_operand_aliasing={{0}: (2, {})} | custom-call | flops 4294967296 | bytes 14680064 | tf_op jit(solution)/shard_map/pallas_call | solution.py:135
  481.7 8.6 %shard_map.84 = (bf16[128,64,1024]{2,1,0:T(8,128)(2,1)}, bf16[32,64,1024]{2,1,0:T(8,128)(2,1)}) custom-call(bf16[16,16,64,128]{3,2,1,0:T(8,128)(2,1)} %all-to-all-done.came_ref, bf16[1024,1024]{1,0:T(8,128)(2,1)S(1)} %bitcast_multiply_fusion.weight_ref, bf16[128,64,1024]{2,1,0:T(8,128)(2,1)} %get-tuple-element.12.refs_0_), custom_call_target="tpu_custom_call", output_to_operand_aliasing={{0}: (2, {})} | custom-call | flops 4294967296 | bytes 14680064 | tf_op jit(solution)/shard_map/pallas_call | solution.py:135
  490.2 28.9 %fusion.27 = f32[32,128]{1,0:T(8,128)S(1)} fusion(bf16[128,64,1024]{2,1,0:T(8,128)(2,1)} %rows_ref.7, bf16[32,64,1024]{2,1,0:T(8,128)(2,1)} %get-tuple-element.17), kind=kOutput, calls=%fused_computation.17 | convolution fusion | flops 536870912 | bytes 20987904 | tf_op jit(solution)/shard_map/dot_general | solution.py:191
  519.1 29.3 %fusion.22 = f32[32,128]{1,0:T(8,128)S(1)} fusion(bf16[128,64,1024]{2,1,0:T(8,128)(2,1)} %rows_ref.7, bf16[32,64,1024]{2,1,0:T(8,128)(2,1)} %get-tuple-element.16), kind=kOutput, calls=%fused_computation.16 | convolution fusion | flops 536870912 | bytes 20987904 | tf_op jit(solution)/shard_map/dot_general | solution.py:191
  548.5 29.1 %fusion.17 = f32[32,128]{1,0:T(8,128)S(1)} fusion(bf16[128,64,1024]{2,1,0:T(8,128)(2,1)} %rows_ref.7, bf16[32,64,1024]{2,1,0:T(8,128)(2,1)} %get-tuple-element.15), kind=kOutput, calls=%fused_computation.15 | convolution fusion | flops 536870912 | bytes 20987904 | tf_op jit(solution)/shard_map/dot_general | solution.py:191
  577.6 29.3 %fusion.12 = f32[32,128]{1,0:T(8,128)S(1)} fusion(bf16[128,64,1024]{2,1,0:T(8,128)(2,1)} %rows_ref.7, bf16[32,64,1024]{2,1,0:T(8,128)(2,1)} %get-tuple-element.14), kind=kOutput, calls=%fused_computation.14 | convolution fusion | flops 536870912 | bytes 20987904 | tf_op jit(solution)/shard_map/dot_general | solution.py:191
  606.9 14.4 %all_to_all.30 = f32[16,8,128]{2,1,0:T(8,128)S(1)} all-to-all(f32[16,8,128]{2,1,0:T(8,128)S(1)} %maximum_bitcast_fusion), channel_id=1, replica_groups=mesh['grp'=2,'row'=8,'col'=2] {'row','col'}, dimensions={0} | all-to-all | bytes 131072 | tf_op jit(solution)/shard_map/all_to_all | solution.py:163
  621.3 9.5 %all_to_all.31 = f32[16,8,128]{2,1,0:T(8,128)S(1)} all-to-all(f32[16,8,128]{2,1,0:T(8,128)S(1)} %broadcast_in_dim.22), channel_id=1, replica_groups=mesh['grp'=2,'row'=8,'col'=2] {'row','col'}, dimensions={0} | all-to-all | bytes 131072 | tf_op jit(solution)/shard_map/all_to_all | solution.py:166
  630.8 0.6 multiply_bitcast_fusion
  (14 shorter events, 0.6 us)
Async XLA Ops:
  7.2 0.8 copy-start
  7.2 47.1 %all-gather.3.cloned.1.call-start = ((), (), s32[]{:S(2)}) async-start(), calls=%async_computation.6 | async-start | bytes 2228224 | tf_op jit(solution)/shard_map/all_gather | solution.py:176
  70.9 82.2 %all-to-all-start.3 = ((bf16[16,16,64,128]{3,2,1,0:T(8,128)(2,1)}), bf16[16,16,64,128]{3,2,1,0:T(8,128)(2,1)}, u32[]{:S(2)}, u32[]{:S(2)}) async-start(bf16[16,16,64,128]{3,2,1,0:T(8,128)(2,1)} %shard_map.80), calls=%async_computation.3 | async-start | bytes 8388608 | tf_op jit(solution)/shard_map/all_to_all | solution.py:185
  153.0 97.4 %all-to-all-start.2 = ((bf16[16,16,64,128]{3,2,1,0:T(8,128)(2,1)}), bf16[16,16,64,128]{3,2,1,0:T(8,128)(2,1)}, u32[]{:S(2)}, u32[]{:S(2)}) async-start(bf16[16,16,64,128]{3,2,1,0:T(8,128)(2,1)} %shard_map.79), calls=%async_computation.2 | async-start | bytes 8388608 | tf_op jit(solution)/shard_map/all_to_all | solution.py:185
  250.4 97.4 %all-to-all-start.1 = ((bf16[16,16,64,128]{3,2,1,0:T(8,128)(2,1)}), bf16[16,16,64,128]{3,2,1,0:T(8,128)(2,1)}, u32[]{:S(2)}, u32[]{:S(2)}) async-start(bf16[16,16,64,128]{3,2,1,0:T(8,128)(2,1)} %shard_map.78), calls=%async_computation.1 | async-start | bytes 8388608 | tf_op jit(solution)/shard_map/all_to_all | solution.py:185
  347.8 133.9 %all-to-all-start = ((bf16[16,16,64,128]{3,2,1,0:T(8,128)(2,1)}), bf16[16,16,64,128]{3,2,1,0:T(8,128)(2,1)}, u32[]{:S(2)}, u32[]{:S(2)}) async-start(bf16[16,16,64,128]{3,2,1,0:T(8,128)(2,1)} %shard_map.77), calls=%async_computation | async-start | bytes 8388608 | tf_op jit(solution)/shard_map/all_to_all | solution.py:185
  367.5 85.1 %all-gather.5.cloned.1.call-start = ((), (), s32[]{:S(2)}) async-start(), calls=%async_computation.7 | async-start | bytes 2228224 | tf_op jit(solution)/shard_map/all_gather | solution.py:177
  577.6 53.9 %copy-start.1 = (s32[1,8,8]{2,1,0:T(8,128)S(1)}, s32[1,8,8]{2,1,0:T(8,128)}, u32[]{:S(2)}) copy-start(s32[1,8,8]{2,1,0:T(8,128)} %param.9) | copy-start | bytes 772
Sparse Core Ops, SparseCore 0:
  10.2 44.0 all-gather.2
  370.5 82.0 all-gather.4

commit v2 on v1

--- a/solution.py
+++ b/solution.py
@@ -8,7 +8,7 @@
 from jax.sharding import PartitionSpec as P
 
 AXES = ("row", "col")
-CHUNKS = 4
+SHARES = (1, 3, 3, 1)
 STEP = 8
 VMEM = 48 * 2**20
 
@@ -97,15 +97,15 @@
     xform_ref[...] = product.astype(jnp.bfloat16).reshape(step, rows, depth)
 
 
-def transform_chunk(weight, three_centre, chunk, chunk_size, owners):
+def transform_chunk(weight, three_centre, first, chunk_size, owners):
     ri_count, rows, depth = three_centre.shape
-    steps = chunk_size // STEP
+    steps, offset = chunk_size // STEP, first // STEP
     return pl.pallas_call(
         first_kernel,
         grid=(steps,),
         in_specs=[
             pl.BlockSpec((depth, depth), lambda i: (0, 0)),
-            pl.BlockSpec((STEP, rows, depth), lambda i: (chunk * steps + i, 0, 0)),
+            pl.BlockSpec((STEP, rows, depth), lambda i: (offset + i, 0, 0)),
         ],
         out_specs=pl.BlockSpec((owners, STEP // 2, rows, 2 * rows), lambda i: (0, i, 0, 0)),
         out_shape=jax.ShapeDtypeStruct((owners, chunk_size // 2, rows, 2 * rows), jnp.bfloat16),
@@ -118,10 +118,10 @@
     )(weight, three_centre)
 
 
-def finish_chunk(came, weight, half, chunk, chunk_size, ri_count):
+def finish_chunk(came, weight, half, first, chunk_size, ri_count):
     owners, pairs, rows, lanes = came.shape
     depth = weight.shape[0]
-    steps = chunk_size // STEP
+    steps, offset = chunk_size // STEP, first // STEP
     operands = [came, weight]
     in_specs = [
         pl.BlockSpec((owners, STEP // 2, rows, lanes), lambda i: (0, i, 0, 0)),
@@ -137,7 +137,7 @@
         grid=(steps,),
         in_specs=in_specs,
         out_specs=[
-            pl.BlockSpec((STEP, rows, depth), lambda i: (chunk * steps + i, 0, 0)),
+            pl.BlockSpec((STEP, rows, depth), lambda i: (offset + i, 0, 0)),
             pl.BlockSpec((STEP, rows, depth), lambda i: (i, 0, 0)),
         ],
         out_shape=[
@@ -170,29 +170,40 @@
 def local_fused(owners, three_centre, green_occ, green_virt, mask_three, mask_occ, mask_virt):
     ri_count, rows, depth = three_centre.shape
     block_size = depth // mask_occ.shape[0]
-    chunk_size = ri_count // CHUNKS
+    sizes = [ri_count // sum(SHARES) * share for share in SHARES]
+    firsts = [sum(sizes[:chunk]) for chunk in range(len(sizes))]
     own_block = lax.axis_index(AXES) * rows // block_size
     own_mask = lax.dynamic_slice_in_dim(mask_three[0], own_block, 1, 0)
-    occ_full = lax.all_gather(green_occ, AXES, axis=0, tiled=True)
-    virt_full = lax.all_gather(green_virt, AXES, axis=0, tiled=True)
+    both = jnp.concatenate([green_occ, green_virt], axis=1)
+    both = lax.all_gather(both, AXES, axis=0, tiled=True)
+    occ_full, virt_full = both[:, :depth], both[:, depth:]
     occ_weight = occ_full.T * spread(mask_occ.T * own_mask, block_size)
     virt_weight = virt_full * spread(mask_virt * own_mask, block_size)
-    sent = [
-        transform_chunk(occ_weight, three_centre, chunk, chunk_size, owners)
-        for chunk in range(CHUNKS)
-    ]
-    came = [
-        lax.all_to_all(block, AXES, split_axis=0, concat_axis=0, tiled=True) for block in sent
-    ]
+    three_flat = lax.optimization_barrier(three_centre.reshape(ri_count, rows * depth))
     half, parts = None, []
-    for chunk in range(CHUNKS):
-        half, xform = finish_chunk(came[chunk], virt_weight, half, chunk, chunk_size, ri_count)
+    came = {}
+
+    def send(chunk):
+        block = transform_chunk(occ_weight, three_centre, firsts[chunk], sizes[chunk], owners)
+        if chunk >= 2:
+            block, came[chunk - 1], parts[chunk - 2] = lax.optimization_barrier(
+                (block, came[chunk - 1], parts[chunk - 2])
+            )
+        elif chunk == 1:
+            block, came[0] = lax.optimization_barrier((block, came[0]))
+        came[chunk] = lax.all_to_all(block, AXES, split_axis=0, concat_axis=0, tiled=True)
+
+    send(0)
+    for chunk in range(len(sizes)):
+        if chunk + 1 < len(sizes):
+            send(chunk + 1)
+        half, xform = finish_chunk(
+            came[chunk], virt_weight, half, firsts[chunk], sizes[chunk], ri_count
+        )
+        flat = lax.optimization_barrier(xform.reshape(sizes[chunk], rows * depth))
         parts.append(
             lax.dot_general(
-                xform,
-                three_centre,
-                (((1, 2), (1, 2)), ((), ())),
-                preferred_element_type=jnp.float32,
+                flat, three_flat, (((1,), (1,)), ((), ())), preferred_element_type=jnp.float32
             )
         )
     response = -sum_over_devices(jnp.concatenate(parts, axis=0), owners) / depth
@@ -208,7 +219,7 @@
         and block_size % rows == 0
         and owners % 2 == 0
         and owners * rows == depth
-        and ri_count % (CHUNKS * STEP) == 0
+        and ri_count % (sum(SHARES) * STEP) == 0
         and ri_count % owners == 0
     )
     body = functools.partial(local_fused, owners) if fits else local_plain

time: 645 us -> 513 us (0.80)
  waiting for transfers between devices: 340 us -> 229 us
  matrix products: 117 us -> 46.2 us
  local copies, waits for them, and re-layouts: 10 us -> 48.4 us
  starting transfers between devices: 64 us -> 72.9 us
    all_gather x2 -> x1, waiting for transfers between devices: 130 us -> 54.1 us  [local_fused(): both = lax.all_gather(both, AXES, axis=0, tiled=True)]
    dot_general x4, matrix products: 117 us -> 46.2 us  [local_fused(): lax.dot_general(flat, three_flat, (((1,), (1,)), ((), ())), preferred_ele...]
    unnamed x4 -> x19, local copies, waits for them, and re-layouts: 0.02 us -> 42.4 us
    all_to_all x4, waiting for transfers between devices: 210 us -> 174 us  [send(): lax.all_to_all(block, AXES, split_axis=0, concat_axis=0, tiled=True)]
    all_to_all x4, starting transfers between devices: 63.6 us -> 72.8 us  [send(): lax.all_to_all(block, AXES, split_axis=0, concat_axis=0, tiled=True)]
  transfers between devices with their start and end apart: 6 -> 5, of which waited for: 5 -> 5; matrix products, arithmetic and copies ran while one was open for 1% -> 16% of each run, Pallas kernels for 7% -> 11%
where the time goes in v2:
time: 513 us; the launch traced here: 508 us
  waiting for transfers between devices  229 us (45%)
  starting transfers between devices  72.9 us (14%)
  Pallas kernels  62.5 us (12%)
  local copies, waits for them, and re-layouts  48.4 us (9%)
  matrix products  46.2 us (9%)
  blocking collectives  27.4 us (5%)
  between operations  14.5 us (3%)
  other arithmetic  7.83 us (2%)
    all_to_all x4, waiting for transfers between devices, send(): lax.all_to_all(block, AXES, split_axis=0, concat_axis=0, tiled=True)  174 us
    all_to_all x4, starting transfers between devices, send(): lax.all_to_all(block, AXES, split_axis=0, concat_axis=0, tiled=True)  72.8 us
    all_gather x1, waiting for transfers between devices, local_fused(): both = lax.all_gather(both, AXES, axis=0, tiled=True)  54.1 us
    dot_general x4, matrix products, local_fused(): lax.dot_general(flat, three_flat, (((1,), (1,)), ((), ())), preferred_ele...  46.2 us
    unnamed x19, local copies, waits for them, and re-layouts  42.4 us
    pallas_call x4, Pallas kernels, finish_chunk(): pl.pallas_call(second_kernel, grid=(steps,), in_specs=in_specs, out_specs...  32.8 us
    pallas_call x4, Pallas kernels, transform_chunk(): pl.pallas_call(first_kernel, grid=(steps,), in_specs=[pl.BlockSpec((depth...  29.7 us
    all_to_all x1, blocking collectives, sum_over_devices(): lax.all_to_all(pieces, AXES, split_axis=0, concat_axis=0, tiled=True)  17.9 us
  transfers between devices with their start and end apart: 5, of which 5 were waited for; matrix products, arithmetic and copies ran while one was open for 16% of the time, Pallas kernels for 11%

profile of v2, /device:TPU:0, one launch (start us, length us, event | category | flops | bytes accessed | tf_op | source)
XLA Modules:
  0.0 508.2 jit_solution(12380881564188682069)
XLA Ops:
  7.2 1.7 pad_maximum_fusion
  9.9 54.1 %all-gather.2.cloned.1.call-done = bf16[1024,2048]{1,0:T(8,128)(2,1)} async-done(((bf16[64,2048]{1,0:T(8,128)(2,1)}), bf16[1024,2048]{1,0:T(8,128)(2,1)}) %all-gather.2.cloned.1.call-update) | async-done | bytes 4194320 | tf_op jit(solution)/shard_map/all_gather | solution.py:178
  64.0 3.1 fusion
  67.1 2.9 copy.12.weight_ref
  70.0 3.9 shard_map.80
  75.2 4.5 all-to-all-start
  79.7 10.8 %shard_map.79 = bf16[16,24,64,128]{3,2,1,0:T(8,128)(2,1)} custom-call(bf16[1024,1024]{1,0:T(8,128)(2,1)S(1)} %copy.12.weight_ref, bf16[128,64,1024]{2,1,0:T(8,128)(2,1)} %rows_ref.7), custom_call_target="tpu_custom_call" | custom-call | flops 6442450944 | bytes 14680064 | tf_op jit(solution)/shard_map/pallas_call | solution.py:103
  90.5 30.3 %all-to-all-done.came_ref = bf16[16,8,64,128]{3,2,1,0:T(8,128)(2,1)} async-done(((bf16[16,8,64,128]{3,2,1,0:T(8,128)(2,1)}), bf16[16,8,64,128]{3,2,1,0:T(8,128)(2,1)}, u32[]{:S(2)}, u32[]{:S(2)}) %all-to-all-start) | async-done | bytes 2097184 | tf_op jit(solution)/shard_map/all_to_all | solution.py:194
  120.8 11.8 %all-to-all-start.1 = ((bf16[16,24,64,128]{3,2,1,0:T(8,128)(2,1)}), bf16[16,24,64,128]{3,2,1,0:T(8,128)(2,1)}, u32[]{:S(2)}, u32[]{:S(2)}) async-start(bf16[16,24,64,128]{3,2,1,0:T(8,128)(2,1)} %shard_map.79), calls=%async_computation.1 | async-start | bytes 12582912 | tf_op jit(solution)/shard_map/all_to_all | solution.py:194
  132.6 18.8 %copy.18 = bf16[16,8,64,1024]{3,1,2,0:T(8,128)(2,1)} copy(bf16[16,8,64,1024]{3,2,1,0:T(8,128)(2,1)} %bitcast.40) | data formatting | bytes 33554432
  151.4 2.9 broadcast_in_dim.21
  154.4 1.6 bitcast_multiply_fusion.weight_ref
  156.0 10.8 %shard_map.78 = bf16[16,24,64,128]{3,2,1,0:T(8,128)(2,1)} custom-call(bf16[1024,1024]{1,0:T(8,128)(2,1)S(1)} %copy.12.weight_ref, bf16[128,64,1024]{2,1,0:T(8,128)(2,1)} %rows_ref.7), custom_call_target="tpu_custom_call" | custom-call | flops 6442450944 | bytes 14680064 | tf_op jit(solution)/shard_map/pallas_call | solution.py:103
  166.8 4.8 shard_map.81
  171.6 2.5 copy.17
  174.2 10.8 %fusion.2 = f32[16,128]{1,0:T(8,128)S(1)} fusion(bf16[16,65536]{1,0:T(8,128)(2,1)} %bitcast.49, bf16[128,65536]{1,0:T(8,128)(2,1)} %bitcast.41), kind=kOutput, calls=%fused_computation.11 | convolution fusion | flops 268435456 | bytes 18882560 | tf_op jit(solution)/shard_map/dot_general | solution.py:205
  185.0 61.8 %all-to-all-done.1.came_ref = bf16[16,24,64,128]{3,2,1,0:T(8,128)(2,1)} async-done(((bf16[16,24,64,128]{3,2,1,0:T(8,128)(2,1)}), bf16[16,24,64,128]{3,2,1,0:T(8,128)(2,1)}, u32[]{:S(2)}, u32[]{:S(2)}) %all-to-all-start.1) | async-done | bytes 6291488 | tf_op jit(solution)/shard_map/all_to_all | solution.py:194
  246.7 28.3 %all-to-all-start.2 = ((bf16[16,24,64,128]{3,2,1,0:T(8,128)(2,1)}), bf16[16,24,64,128]{3,2,1,0:T(8,128)(2,1)}, u32[]{:S(2)}, u32[]{:S(2)}) async-start(bf16[16,24,64,128]{3,2,1,0:T(8,128)(2,1)} %shard_map.78), calls=%async_computation.2 | async-start | bytes 12582912 | tf_op jit(solution)/shard_map/all_to_all | solution.py:194
  275.0 4.1 shard_map.77
  279.2 12.0 %shard_map.82 = (bf16[128,64,1024]{2,1,0:T(8,128)(2,1)}, bf16[48,64,1024]{2,1,0:T(8,128)(2,1)}) custom-call(bf16[16,24,64,128]{3,2,1,0:T(8,128)(2,1)} %all-to-all-done.1.came_ref, bf16[1024,1024]{1,0:T(8,128)(2,1)S(1)} %copy-done.2, bf16[128,64,1024]{2,1,0:T(8,128)(2,1)} %get-tuple-element.23.refs_0_), custom_call_target="tpu_custom_call", output_to_operand_aliasing={{0}: (2, {})} | custom-call | flops 6442450944 | bytes 20971520 | tf_op jit(solution)/shard_map/pallas_call | solution.py:135
  291.2 9.3 %copy.19 = bf16[6,8,64,1024]{3,1,2,0:T(8,128)(2,1)} copy(bf16[6,8,64,1024]{3,2,1,0:T(8,128)(2,1)} %bitcast.50) | data formatting | bytes 12582912
  300.5 13.6 %fusion.3 = f32[48,128]{1,0:T(8,128)S(1)} fusion(bf16[48,65536]{1,0:T(8,128)(2,1)} %bitcast.45, bf16[128,65536]{1,0:T(8,128)(2,1)} %bitcast.42), kind=kOutput, calls=%fused_computation.12 | convolution fusion | flops 805306368 | bytes 23093248 | tf_op jit(solution)/shard_map/dot_general | solution.py:205
  314.1 75.1 %all-to-all-done.2.came_ref = bf16[16,24,64,128]{3,2,1,0:T(8,128)(2,1)} async-done(((bf16[16,24,64,128]{3,2,1,0:T(8,128)(2,1)}), bf16[16,24,64,128]{3,2,1,0:T(8,128)(2,1)}, u32[]{:S(2)}, u32[]{:S(2)}) %all-to-all-start.2) | async-done | bytes 6291488 | tf_op jit(solution)/shard_map/all_to_all | solution.py:194
  389.2 28.3 %all-to-all-start.3 = ((bf16[16,8,64,128]{3,2,1,0:T(8,128)(2,1)}), bf16[16,8,64,128]{3,2,1,0:T(8,128)(2,1)}, u32[]{:S(2)}, u32[]{:S(2)}) async-start(bf16[16,8,64,128]{3,2,1,0:T(8,128)(2,1)} %copy-done.4), calls=%async_computation.3 | async-start | bytes 4194304 | tf_op jit(solution)/shard_map/all_to_all | solution.py:194
  417.6 11.2 %shard_map.83 = (bf16[128,64,1024]{2,1,0:T(8,128)(2,1)}, bf16[48,64,1024]{2,1,0:T(8,128)(2,1)}) custom-call(bf16[16,24,64,128]{3,2,1,0:T(8,128)(2,1)} %all-to-all-done.2.came_ref, bf16[1024,1024]{1,0:T(8,128)(2,1)S(1)} %copy-done.3, bf16[128,64,1024]{2,1,0:T(8,128)(2,1)} %get-tuple-element.27.refs_0_), custom_call_target="tpu_custom_call", output_to_operand_aliasing={{0}: (2, {})} | custom-call | flops 6442450944 | bytes 20971520 | tf_op jit(solution)/shard_map/pallas_call | solution.py:135
  428.8 9.2 %copy.20 = bf16[6,8,64,1024]{3,1,2,0:T(8,128)(2,1)} copy(bf16[6,8,64,1024]{3,2,1,0:T(8,128)(2,1)} %bitcast.51) | data formatting | bytes 12582912
  438.0 13.4 %fusion.4 = f32[48,128]{1,0:T(8,128)S(1)} fusion(bf16[48,65536]{1,0:T(8,128)(2,1)} %bitcast.46, bf16[128,65536]{1,0:T(8,128)(2,1)} %bitcast.43), kind=kOutput, calls=%fused_computation.13 | convolution fusion | flops 805306368 | bytes 23093248 | tf_op jit(solution)/shard_map/dot_general | solution.py:205
  451.5 7.2 %all-to-all-done.3.came_ref = bf16[16,8,64,128]{3,2,1,0:T(8,128)(2,1)} async-done(((bf16[16,8,64,128]{3,2,1,0:T(8,128)(2,1)}), bf16[16,8,64,128]{3,2,1,0:T(8,128)(2,1)}, u32[]{:S(2)}, u32[]{:S(2)}) %all-to-all-start.3) | async-done | bytes 2097184 | tf_op jit(solution)/shard_map/all_to_all | solution.py:194
  458.7 4.8 shard_map.84
  464.7 8.3 %fusion.5 = f32[16,128]{1,0:T(8,128)S(1)} fusion(bf16[16,65536]{1,0:T(8,128)(2,1)S(1)} %bitcast.48, bf16[128,65536]{1,0:T(8,128)(2,1)} %bitcast.44), kind=kOutput, calls=%fused_computation.14 | convolution fusion | flops 268435456 | bytes 18882560 | tf_op jit(solution)/shard_map/dot_general | solution.py:205
  473.0 17.9 %all_to_all.30 = f32[16,8,128]{2,1,0:T(8,128)S(1)} all-to-all(f32[16,8,128]{2,1,0:T(8,128)S(1)} %maximum_bitcast_fusion), channel_id=1, replica_groups=mesh['grp'=2,'row'=8,'col'=2] {'row','col'}, dimensions={0} | all-to-all | bytes 131072 | tf_op jit(solution)/shard_map/all_to_all | solution.py:163
  490.9 9.5 %all_to_all.31 = f32[16,8,128]{2,1,0:T(8,128)S(1)} all-to-all(f32[16,8,128]{2,1,0:T(8,128)S(1)} %broadcast_in_dim.22), channel_id=1, replica_groups=mesh['grp'=2,'row'=8,'col'=2] {'row','col'}, dimensions={0} | all-to-all | bytes 131072 | tf_op jit(solution)/shard_map/all_to_all | solution.py:166
  (26 shorter events, 4.2 us)
Async XLA Ops:
  7.2 1.8 copy-start
  7.2 56.9 %all-gather.2.cloned.1.call-start = ((), (), s32[]{:S(2)}) async-start(), calls=%async_computation.6 | async-start | bytes 4456448 | tf_op jit(solution)/shard_map/all_gather | solution.py:178
  73.9 1.3 copy-start.5
  75.2 45.5 %all-to-all-start = ((bf16[16,8,64,128]{3,2,1,0:T(8,128)(2,1)}), bf16[16,8,64,128]{3,2,1,0:T(8,128)(2,1)}, u32[]{:S(2)}, u32[]{:S(2)}) async-start(bf16[16,8,64,128]{3,2,1,0:T(8,128)(2,1)} %copy-done.5), calls=%async_computation | async-start | bytes 4194304 | tf_op jit(solution)/shard_map/all_to_all | solution.py:194
  120.8 126.0 %all-to-all-start.1 = ((bf16[16,24,64,128]{3,2,1,0:T(8,128)(2,1)}), bf16[16,24,64,128]{3,2,1,0:T(8,128)(2,1)}, u32[]{:S(2)}, u32[]{:S(2)}) async-start(bf16[16,24,64,128]{3,2,1,0:T(8,128)(2,1)} %shard_map.79), calls=%async_computation.1 | async-start | bytes 12582912 | tf_op jit(solution)/shard_map/all_to_all | solution.py:194
  132.6 21.8 %copy-start.6 = (bf16[1024,2048]{1,0:T(8,128)(2,1)S(1)}, bf16[1024,2048]{1,0:T(8,128)(2,1)}, u32[]{:S(2)}) copy-start(bf16[1024,2048]{1,0:T(8,128)(2,1)} %all-gather.2.cloned.1.call-done) | copy-start | bytes 12582916
  246.7 142.5 %all-to-all-start.2 = ((bf16[16,24,64,128]{3,2,1,0:T(8,128)(2,1)}), bf16[16,24,64,128]{3,2,1,0:T(8,128)(2,1)}, u32[]{:S(2)}, u32[]{:S(2)}) async-start(bf16[16,24,64,128]{3,2,1,0:T(8,128)(2,1)} %shard_map.78), calls=%async_computation.2 | async-start | bytes 12582912 | tf_op jit(solution)/shard_map/all_to_all | solution.py:194
  275.0 4.1 copy-start.2
  279.2 12.1 %copy-start.4 = (bf16[16,8,64,128]{3,2,1,0:T(8,128)(2,1)}, bf16[16,8,64,128]{3,2,1,0:T(8,128)(2,1)S(1)}, u32[]{:S(2)}) copy-start(bf16[16,8,64,128]{3,2,1,0:T(8,128)(2,1)S(1)} %shard_map.77) | copy-start | bytes 6291460
  300.5 117.1 %copy-start.3 = (bf16[1024,1024]{1,0:T(8,128)(2,1)S(1)}, bf16[1024,1024]{1,0:T(8,128)(2,1)}, u32[]{:S(2)}) copy-start(bf16[1024,1024]{1,0:T(8,128)(2,1)} %bitcast_multiply_fusion.weight_ref) | copy-start | bytes 6291460
  389.2 69.5 %all-to-all-start.3 = ((bf16[16,8,64,128]{3,2,1,0:T(8,128)(2,1)}), bf16[16,8,64,128]{3,2,1,0:T(8,128)(2,1)}, u32[]{:S(2)}, u32[]{:S(2)}) async-start(bf16[16,8,64,128]{3,2,1,0:T(8,128)(2,1)} %copy-done.4), calls=%async_computation.3 | async-start | bytes 4194304 | tf_op jit(solution)/shard_map/all_to_all | solution.py:194
  464.6 36.4 %copy-start.1 = (s32[1,8,8]{2,1,0:T(8,128)S(1)}, s32[1,8,8]{2,1,0:T(8,128)}, u32[]{:S(2)}) copy-start(s32[1,8,8]{2,1,0:T(8,128)} %param.9) | copy-start | bytes 772
Sparse Core Ops, SparseCore 0:
  10.8 53.2 all-gather.1

commit v3 on v2

--- a/solution.py
+++ b/solution.py
@@ -174,9 +174,8 @@
     firsts = [sum(sizes[:chunk]) for chunk in range(len(sizes))]
     own_block = lax.axis_index(AXES) * rows // block_size
     own_mask = lax.dynamic_slice_in_dim(mask_three[0], own_block, 1, 0)
-    both = jnp.concatenate([green_occ, green_virt], axis=1)
-    both = lax.all_gather(both, AXES, axis=0, tiled=True)
-    occ_full, virt_full = both[:, :depth], both[:, depth:]
+    occ_full = lax.all_gather(green_occ, AXES, axis=0, tiled=True)
+    virt_full = lax.all_gather(green_virt, AXES, axis=0, tiled=True)
     occ_weight = occ_full.T * spread(mask_occ.T * own_mask, block_size)
     virt_weight = virt_full * spread(mask_virt * own_mask, block_size)
     three_flat = lax.optimization_barrier(three_centre.reshape(ri_count, rows * depth))

time: 513 us -> 526 us (1.025)
  waiting for transfers between devices: 229 us -> 252 us
  starting transfers between devices: 72.9 us -> 59.4 us
    all_gather x1 -> x2, waiting for transfers between devices: 54.1 us -> 139 us  [the longest x1 93.1 us: local_fused(): virt_full = lax.all_gather(green_virt, AXES, axis=0, tiled=True)]
    all_to_all x4, waiting for transfers between devices: 174 us -> 113 us  [send(): lax.all_to_all(block, AXES, split_axis=0, concat_axis=0, tiled=True)]
    all_to_all x4, starting transfers between devices: 72.8 us -> 58.8 us  [send(): lax.all_to_all(block, AXES, split_axis=0, concat_axis=0, tiled=True)]
    unnamed x19 -> x17, local copies, waits for them, and re-layouts: 42.4 us -> 42.2 us
  transfers between devices with their start and end apart: 5 -> 6, of which waited for: 5 -> 5; matrix products, arithmetic and copies ran while one was open for 16% -> 16% of each run, Pallas kernels for 11% -> 10%
where the time goes in v3:
time: 526 us; the launch traced here: 521 us
  waiting for transfers between devices  252 us (48%)
  Pallas kernels  62.5 us (12%)
  starting transfers between devices  59.4 us (11%)
  local copies, waits for them, and re-layouts  52.2 us (10%)
  matrix products  46.2 us (9%)
  blocking collectives  27.4 us (5%)
  between operations  14.5 us (3%)
  other arithmetic  6.54 us (1%)
    all_to_all x4, waiting for transfers between devices, send(): lax.all_to_all(block, AXES, split_axis=0, concat_axis=0, tiled=True)  113 us
    all_gather x1, waiting for transfers between devices, local_fused(): virt_full = lax.all_gather(green_virt, AXES, axis=0, tiled=True)  93.1 us
    all_to_all x4, starting transfers between devices, send(): lax.all_to_all(block, AXES, split_axis=0, concat_axis=0, tiled=True)  58.8 us
    dot_general x4, matrix products, local_fused(): lax.dot_general(flat, three_flat, (((1,), (1,)), ((), ())), preferred_ele...  46.2 us
    all_gather x1, waiting for transfers between devices, local_fused(): occ_full = lax.all_gather(green_occ, AXES, axis=0, tiled=True)  45.5 us
    unnamed x17, local copies, waits for them, and re-layouts  42.2 us
    pallas_call x4, Pallas kernels, finish_chunk(): pl.pallas_call(second_kernel, grid=(steps,), in_specs=in_specs, out_specs...  32.9 us
    pallas_call x4, Pallas kernels, transform_chunk(): pl.pallas_call(first_kernel, grid=(steps,), in_specs=[pl.BlockSpec((depth...  29.6 us
  transfers between devices with their start and end apart: 6, of which 5 were waited for; matrix products, arithmetic and copies ran while one was open for 16% of the time, Pallas kernels for 10%

profile of v3, /device:TPU:0, one launch (start us, length us, event | category | flops | bytes accessed | tf_op | source)
XLA Modules:
  0.0 520.8 jit_solution(16950247310782862809)
XLA Ops:
  8.8 45.5 %all-gather.3.cloned.1.call-done = bf16[1024,1024]{1,0:T(8,128)(2,1)} async-done(((bf16[64,1024]{1,0:T(8,128)(2,1)}), bf16[1024,1024]{1,0:T(8,128)(2,1)}) %all-gather.3.cloned.1.call-update) | async-done | bytes 2097168 | tf_op jit(solution)/shard_map/all_gather | solution.py:177
  54.3 3.9 copy.13
  58.3 2.9 broadcast_in_dim.19
  61.2 1.9 bitcast_multiply_fusion.1.weight_ref
  63.1 3.9 shard_map.80
  68.4 4.4 all-to-all-start
  72.8 10.8 %shard_map.79 = bf16[16,24,64,128]{3,2,1,0:T(8,128)(2,1)} custom-call(bf16[1024,1024]{1,0:T(8,128)(2,1)S(1)} %bitcast_multiply_fusion.1.weight_ref, bf16[128,64,1024]{2,1,0:T(8,128)(2,1)} %rows_ref.7), custom_call_target="tpu_custom_call" | custom-call | flops 6442450944 | bytes 14680064 | tf_op jit(solution)/shard_map/pallas_call | solution.py:103
  83.6 30.3 %all-to-all-done.came_ref = bf16[16,8,64,128]{3,2,1,0:T(8,128)(2,1)} async-done(((bf16[16,8,64,128]{3,2,1,0:T(8,128)(2,1)}), bf16[16,8,64,128]{3,2,1,0:T(8,128)(2,1)}, u32[]{:S(2)}, u32[]{:S(2)}) %all-to-all-start) | async-done | bytes 2097184 | tf_op jit(solution)/shard_map/all_to_all | solution.py:193
  113.9 11.2 %all-to-all-start.1 = ((bf16[16,24,64,128]{3,2,1,0:T(8,128)(2,1)}), bf16[16,24,64,128]{3,2,1,0:T(8,128)(2,1)}, u32[]{:S(2)}, u32[]{:S(2)}) async-start(bf16[16,24,64,128]{3,2,1,0:T(8,128)(2,1)} %shard_map.79), calls=%async_computation.1 | async-start | bytes 12582912 | tf_op jit(solution)/shard_map/all_to_all | solution.py:193
  125.9 18.7 %copy.18 = bf16[16,8,64,1024]{3,1,2,0:T(8,128)(2,1)} copy(bf16[16,8,64,1024]{3,2,1,0:T(8,128)(2,1)} %bitcast.38) | data formatting | bytes 33554432
  144.6 93.1 %all-gather.5.cloned.1.call-done = bf16[1024,1024]{1,0:T(8,128)(2,1)} async-done(((bf16[64,1024]{1,0:T(8,128)(2,1)}), bf16[1024,1024]{1,0:T(8,128)(2,1)}) %all-gather.5.cloned.1.call-update) | async-done | bytes 2097168 | tf_op jit(solution)/shard_map/all_gather | solution.py:178
  237.7 2.9 broadcast_in_dim.21
  240.7 3.2 bitcast_multiply_fusion.weight_ref
  243.9 10.8 %shard_map.78 = bf16[16,24,64,128]{3,2,1,0:T(8,128)(2,1)} custom-call(bf16[1024,1024]{1,0:T(8,128)(2,1)S(1)} %bitcast_multiply_fusion.1.weight_ref, bf16[128,64,1024]{2,1,0:T(8,128)(2,1)} %rows_ref.7), custom_call_target="tpu_custom_call" | custom-call | flops 6442450944 | bytes 14680064 | tf_op jit(solution)/shard_map/pallas_call | solution.py:103
  254.7 4.8 shard_map.81
  259.5 2.5 copy.17
  262.0 10.8 %fusion.1 = f32[16,128]{1,0:T(8,128)S(1)} fusion(bf16[16,65536]{1,0:T(8,128)(2,1)} %bitcast.48, bf16[128,65536]{1,0:T(8,128)(2,1)} %bitcast.39), kind=kOutput, calls=%fused_computation.8 | convolution fusion | flops 268435456 | bytes 18882560 | tf_op jit(solution)/shard_map/dot_general | solution.py:204
  272.8 14.1 %all-to-all-start.2 = ((bf16[16,24,64,128]{3,2,1,0:T(8,128)(2,1)}), bf16[16,24,64,128]{3,2,1,0:T(8,128)(2,1)}, u32[]{:S(2)}, u32[]{:S(2)}) async-start(bf16[16,24,64,128]{3,2,1,0:T(8,128)(2,1)} %shard_map.78), calls=%async_computation.2 | async-start | bytes 12582912 | tf_op jit(solution)/shard_map/all_to_all | solution.py:193
  286.9 4.1 shard_map.77
  291.0 12.0 %shard_map.82 = (bf16[128,64,1024]{2,1,0:T(8,128)(2,1)}, bf16[48,64,1024]{2,1,0:T(8,128)(2,1)}) custom-call(bf16[16,24,64,128]{3,2,1,0:T(8,128)(2,1)} %all-to-all-done.1.came_ref, bf16[1024,1024]{1,0:T(8,128)(2,1)S(1)} %copy-done.2, bf16[128,64,1024]{2,1,0:T(8,128)(2,1)} %get-tuple-element.23.refs_0_), custom_call_target="tpu_custom_call", output_to_operand_aliasing={{0}: (2, {})} | custom-call | flops 6442450944 | bytes 20971520 | tf_op jit(solution)/shard_map/pallas_call | solution.py:135
  303.1 9.3 %copy.19 = bf16[6,8,64,1024]{3,1,2,0:T(8,128)(2,1)} copy(bf16[6,8,64,1024]{3,2,1,0:T(8,128)(2,1)} %bitcast.49) | data formatting | bytes 12582912
  312.4 13.6 %fusion.2 = f32[48,128]{1,0:T(8,128)S(1)} fusion(bf16[48,65536]{1,0:T(8,128)(2,1)} %bitcast.43, bf16[128,65536]{1,0:T(8,128)(2,1)} %bitcast.40), kind=kOutput, calls=%fused_computation.9 | convolution fusion | flops 805306368 | bytes 23093248 | tf_op jit(solution)/shard_map/dot_general | solution.py:204
  326.0 75.1 %all-to-all-done.2.came_ref = bf16[16,24,64,128]{3,2,1,0:T(8,128)(2,1)} async-done(((bf16[16,24,64,128]{3,2,1,0:T(8,128)(2,1)}), bf16[16,24,64,128]{3,2,1,0:T(8,128)(2,1)}, u32[]{:S(2)}, u32[]{:S(2)}) %all-to-all-start.2) | async-done | bytes 6291488 | tf_op jit(solution)/shard_map/all_to_all | solution.py:193
  401.1 29.1 %all-to-all-start.3 = ((bf16[16,8,64,128]{3,2,1,0:T(8,128)(2,1)}), bf16[16,8,64,128]{3,2,1,0:T(8,128)(2,1)}, u32[]{:S(2)}, u32[]{:S(2)}) async-start(bf16[16,8,64,128]{3,2,1,0:T(8,128)(2,1)} %copy-done.4), calls=%async_computation.3 | async-start | bytes 4194304 | tf_op jit(solution)/shard_map/all_to_all | solution.py:193
  430.2 11.2 %shard_map.83 = (bf16[128,64,1024]{2,1,0:T(8,128)(2,1)}, bf16[48,64,1024]{2,1,0:T(8,128)(2,1)}) custom-call(bf16[16,24,64,128]{3,2,1,0:T(8,128)(2,1)} %all-to-all-done.2.came_ref, bf16[1024,1024]{1,0:T(8,128)(2,1)S(1)} %copy-done.3, bf16[128,64,1024]{2,1,0:T(8,128)(2,1)} %get-tuple-element.27.refs_0_), custom_call_target="tpu_custom_call", output_to_operand_aliasing={{0}: (2, {})} | custom-call | flops 6442450944 | bytes 20971520 | tf_op jit(solution)/shard_map/pallas_call | solution.py:135
  441.4 9.2 %copy.20 = bf16[6,8,64,1024]{3,1,2,0:T(8,128)(2,1)} copy(bf16[6,8,64,1024]{3,2,1,0:T(8,128)(2,1)} %bitcast.50) | data formatting | bytes 12582912
  450.6 13.4 %fusion.3 = f32[48,128]{1,0:T(8,128)S(1)} fusion(bf16[48,65536]{1,0:T(8,128)(2,1)} %bitcast.44, bf16[128,65536]{1,0:T(8,128)(2,1)} %bitcast.41), kind=kOutput, calls=%fused_computation.10 | convolution fusion | flops 805306368 | bytes 23093248 | tf_op jit(solution)/shard_map/dot_general | solution.py:204
  464.1 7.2 %all-to-all-done.3.came_ref = bf16[16,8,64,128]{3,2,1,0:T(8,128)(2,1)} async-done(((bf16[16,8,64,128]{3,2,1,0:T(8,128)(2,1)}), bf16[16,8,64,128]{3,2,1,0:T(8,128)(2,1)}, u32[]{:S(2)}, u32[]{:S(2)}) %all-to-all-start.3) | async-done | bytes 2097184 | tf_op jit(solution)/shard_map/all_to_all | solution.py:193
  471.3 4.8 shard_map.84
  477.3 8.3 %fusion.4 = f32[16,128]{1,0:T(8,128)S(1)} fusion(bf16[16,65536]{1,0:T(8,128)(2,1)S(1)} %bitcast.47, bf16[128,65536]{1,0:T(8,128)(2,1)} %bitcast.42), kind=kOutput, calls=%fused_computation.11 | convolution fusion | flops 268435456 | bytes 18882560 | tf_op jit(solution)/shard_map/dot_general | solution.py:204
  485.6 17.9 %all_to_all.30 = f32[16,8,128]{2,1,0:T(8,128)S(1)} all-to-all(f32[16,8,128]{2,1,0:T(8,128)S(1)} %maximum_bitcast_fusion), channel_id=1, replica_groups=mesh['grp'=2,'row'=8,'col'=2] {'row','col'}, dimensions={0} | all-to-all | bytes 131072 | tf_op jit(solution)/shard_map/all_to_all | solution.py:163
  503.6 9.5 %all_to_all.31 = f32[16,8,128]{2,1,0:T(8,128)S(1)} all-to-all(f32[16,8,128]{2,1,0:T(8,128)S(1)} %broadcast_in_dim.22), channel_id=1, replica_groups=mesh['grp'=2,'row'=8,'col'=2] {'row','col'}, dimensions={0} | all-to-all | bytes 131072 | tf_op jit(solution)/shard_map/all_to_all | solution.py:166
  (27 shorter events, 5.6 us)
Async XLA Ops:
  7.2 0.8 copy-start
  7.2 47.1 %all-gather.3.cloned.1.call-start = ((), (), s32[]{:S(2)}) async-start(), calls=%async_computation.6 | async-start | bytes 2228224 | tf_op jit(solution)/shard_map/all_gather | solution.py:177
  67.1 1.3 copy-start.5
  68.4 45.5 %all-to-all-start = ((bf16[16,8,64,128]{3,2,1,0:T(8,128)(2,1)}), bf16[16,8,64,128]{3,2,1,0:T(8,128)(2,1)}, u32[]{:S(2)}, u32[]{:S(2)}) async-start(bf16[16,8,64,128]{3,2,1,0:T(8,128)(2,1)} %copy-done.5), calls=%async_computation | async-start | bytes 4194304 | tf_op jit(solution)/shard_map/all_to_all | solution.py:193
  113.9 158.9 %all-to-all-start.1 = ((bf16[16,24,64,128]{3,2,1,0:T(8,128)(2,1)}), bf16[16,24,64,128]{3,2,1,0:T(8,128)(2,1)}, u32[]{:S(2)}, u32[]{:S(2)}) async-start(bf16[16,24,64,128]{3,2,1,0:T(8,128)(2,1)} %shard_map.79), calls=%async_computation.1 | async-start | bytes 12582912 | tf_op jit(solution)/shard_map/all_to_all | solution.py:193
  125.2 112.5 %all-gather.5.cloned.1.call-start = ((), (), s32[]{:S(2)}) async-start(), calls=%async_computation.7 | async-start | bytes 2228224 | tf_op jit(solution)/shard_map/all_gather | solution.py:178
  272.8 128.2 %all-to-all-start.2 = ((bf16[16,24,64,128]{3,2,1,0:T(8,128)(2,1)}), bf16[16,24,64,128]{3,2,1,0:T(8,128)(2,1)}, u32[]{:S(2)}, u32[]{:S(2)}) async-start(bf16[16,24,64,128]{3,2,1,0:T(8,128)(2,1)} %shard_map.78), calls=%async_computation.2 | async-start | bytes 12582912 | tf_op jit(solution)/shard_map/all_to_all | solution.py:193
  286.9 4.1 copy-start.2
  291.0 12.1 %copy-start.4 = (bf16[16,8,64,128]{3,2,1,0:T(8,128)(2,1)}, bf16[16,8,64,128]{3,2,1,0:T(8,128)(2,1)S(1)}, u32[]{:S(2)}) copy-start(bf16[16,8,64,128]{3,2,1,0:T(8,128)(2,1)S(1)} %shard_map.77) | copy-start | bytes 6291460
  312.4 117.8 %copy-start.3 = (bf16[1024,1024]{1,0:T(8,128)(2,1)S(1)}, bf16[1024,1024]{1,0:T(8,128)(2,1)}, u32[]{:S(2)}) copy-start(bf16[1024,1024]{1,0:T(8,128)(2,1)} %bitcast_multiply_fusion.weight_ref) | copy-start | bytes 6291460
  401.1 70.2 %all-to-all-start.3 = ((bf16[16,8,64,128]{3,2,1,0:T(8,128)(2,1)}), bf16[16,8,64,128]{3,2,1,0:T(8,128)(2,1)}, u32[]{:S(2)}, u32[]{:S(2)}) async-start(bf16[16,8,64,128]{3,2,1,0:T(8,128)(2,1)} %copy-done.4), calls=%async_computation.3 | async-start | bytes 4194304 | tf_op jit(solution)/shard_map/all_to_all | solution.py:193
  477.3 36.4 %copy-start.1 = (s32[1,8,8]{2,1,0:T(8,128)S(1)}, s32[1,8,8]{2,1,0:T(8,128)}, u32[]{:S(2)}) copy-start(s32[1,8,8]{2,1,0:T(8,128)} %param.9) | copy-start | bytes 772
Sparse Core Ops, SparseCore 0:
  10.2 44.0 all-gather.2
  128.2 109.4 all-gather.4

commit v4 on v2

--- a/solution.py
+++ b/solution.py
@@ -8,7 +8,7 @@
 from jax.sharding import PartitionSpec as P
 
 AXES = ("row", "col")
-SHARES = (1, 3, 3, 1)
+SHARES = (2, 11, 3)
 STEP = 8
 VMEM = 48 * 2**20
 

time: 513 us -> 502 us (0.979)
  waiting for transfers between devices: 229 us -> 253 us
  matrix products: 46.2 us -> 28.1 us
  starting transfers between devices: 72.9 us -> 64.9 us
  local copies, waits for them, and re-layouts: 48.4 us -> 42.8 us
    all_to_all x4 -> x3, waiting for transfers between devices: 174 us -> 199 us  [send(): lax.all_to_all(block, AXES, split_axis=0, concat_axis=0, tiled=True)]
    dot_general x4 -> x3, matrix products: 46.2 us -> 28.1 us  [local_fused(): lax.dot_general(flat, three_flat, (((1,), (1,)), ((), ())), preferred_ele...]
    all_to_all x4 -> x3, starting transfers between devices: 72.8 us -> 64.9 us  [send(): lax.all_to_all(block, AXES, split_axis=0, concat_axis=0, tiled=True)]
    unnamed x19 -> x14, local copies, waits for them, and re-layouts: 42.4 us -> 36.8 us
    pallas_call x4 -> x3, Pallas kernels: 32.8 us -> 29.5 us  [finish_chunk(): pl.pallas_call(second_kernel, grid=(steps,), in_specs=in_specs, out_specs...]
    pallas_call x4 -> x3, Pallas kernels: 29.7 us -> 28.7 us  [transform_chunk(): pl.pallas_call(first_kernel, grid=(steps,), in_specs=[pl.BlockSpec((depth...]
  transfers between devices with their start and end apart: 5 -> 4, of which waited for: 5 -> 4; matrix products, arithmetic and copies ran while one was open for 16% -> 12% of each run, Pallas kernels for 11% -> 10%
where the time goes in v4:
time: 502 us; the launch traced here: 501 us
  waiting for transfers between devices  253 us (50%)
  starting transfers between devices  64.9 us (13%)
  Pallas kernels  58.2 us (12%)
  local copies, waits for them, and re-layouts  42.8 us (9%)
  blocking collectives  31.6 us (6%)
  matrix products  28.1 us (6%)
  between operations  14.2 us (3%)
  other arithmetic  7.84 us (2%)
    all_to_all x3, waiting for transfers between devices, send(): lax.all_to_all(block, AXES, split_axis=0, concat_axis=0, tiled=True)  199 us
    all_to_all x3, starting transfers between devices, send(): lax.all_to_all(block, AXES, split_axis=0, concat_axis=0, tiled=True)  64.9 us
    all_gather x1, waiting for transfers between devices, local_fused(): both = lax.all_gather(both, AXES, axis=0, tiled=True)  54.1 us
    unnamed x14, local copies, waits for them, and re-layouts  36.8 us
    pallas_call x3, Pallas kernels, finish_chunk(): pl.pallas_call(second_kernel, grid=(steps,), in_specs=in_specs, out_specs...  29.5 us
    pallas_call x3, Pallas kernels, transform_chunk(): pl.pallas_call(first_kernel, grid=(steps,), in_specs=[pl.BlockSpec((depth...  28.7 us
    dot_general x3, matrix products, local_fused(): lax.dot_general(flat, three_flat, (((1,), (1,)), ((), ())), preferred_ele...  28.1 us
    all_to_all x1, blocking collectives, sum_over_devices(): lax.all_to_all(pieces, AXES, split_axis=0, concat_axis=0, tiled=True)  22.1 us
  transfers between devices with their start and end apart: 4, of which 4 were waited for; matrix products, arithmetic and copies ran while one was open for 12% of the time, Pallas kernels for 10%

profile of v4, /device:TPU:0, one launch (start us, length us, event | category | flops | bytes accessed | tf_op | source)
XLA Modules:
  0.0 500.6 jit_solution(16314966621841423297)
XLA Ops:
  7.2 1.7 pad_maximum_fusion
  9.0 0.8 multiply_convert_fusion
  9.8 0.1 copy.10
  9.9 0.1 broadcast_bitcast_fusion
  9.9 54.1 %all-gather.2.cloned.1.call-done = bf16[1024,2048]{1,0:T(8,128)(2,1)} async-done(((bf16[64,2048]{1,0:T(8,128)(2,1)}), bf16[1024,2048]{1,0:T(8,128)(2,1)}) %all-gather.2.cloned.1.call-update) | async-done | bytes 4194320 | tf_op jit(solution)/shard_map/all_gather | solution.py:178
  64.0 3.1 fusion
  67.1 2.9 copy.11.weight_ref
  70.0 3.9 shard_map.79
  73.9 1.3 copy-done.2
  75.2 4.4 all-to-all-start
  79.7 18.2 %shard_map.78 = bf16[16,44,64,128]{3,2,1,0:T(8,128)(2,1)} custom-call(bf16[1024,1024]{1,0:T(8,128)(2,1)S(1)} %copy.11.weight_ref, bf16[128,64,1024]{2,1,0:T(8,128)(2,1)} %rows_ref.5), custom_call_target="tpu_custom_call" | custom-call | flops 11811160064 | bytes 25165824 | tf_op jit(solution)/shard_map/pallas_call | solution.py:103
  97.9 22.9 %all-to-all-done.came_ref = bf16[16,8,64,128]{3,2,1,0:T(8,128)(2,1)} async-done(((bf16[16,8,64,128]{3,2,1,0:T(8,128)(2,1)}), bf16[16,8,64,128]{3,2,1,0:T(8,128)(2,1)}, u32[]{:S(2)}, u32[]{:S(2)}) %all-to-all-start) | async-done | bytes 2097184 | tf_op jit(solution)/shard_map/all_to_all | solution.py:194
  120.8 11.2 %all-to-all-start.1 = ((bf16[16,44,64,128]{3,2,1,0:T(8,128)(2,1)}), bf16[16,44,64,128]{3,2,1,0:T(8,128)(2,1)}, u32[]{:S(2)}, u32[]{:S(2)}) async-start(bf16[16,44,64,128]{3,2,1,0:T(8,128)(2,1)} %shard_map.78), calls=%async_computation.1 | async-start | bytes 23068672 | tf_op jit(solution)/shard_map/all_to_all | solution.py:194
  132.0 18.6 %copy.16 = bf16[16,8,64,1024]{3,1,2,0:T(8,128)(2,1)} copy(bf16[16,8,64,1024]{3,2,1,0:T(8,128)(2,1)} %bitcast.39) | data formatting | bytes 33554432
  150.6 6.6 %shard_map.77 = bf16[16,12,64,128]{3,2,1,0:T(8,128)(2,1)} custom-call(bf16[1024,1024]{1,0:T(8,128)(2,1)S(1)} %copy.11.weight_ref, bf16[128,64,1024]{2,1,0:T(8,128)(2,1)} %rows_ref.5), custom_call_target="tpu_custom_call" | custom-call | flops 3221225472 | bytes 8388608 | tf_op jit(solution)/shard_map/pallas_call | solution.py:103
  157.3 2.9 broadcast_in_dim.21
  160.2 1.7 bitcast_multiply_fusion.weight_ref
  161.9 4.8 shard_map.80
  166.7 1.2 copy.15
  167.8 8.1 %fusion.2 = f32[16,128]{1,0:T(8,128)S(1)} fusion(bf16[16,65536]{1,0:T(8,128)(2,1)S(1)} %bitcast.44, bf16[128,65536]{1,0:T(8,128)(2,1)} %bitcast.36), kind=kOutput, calls=%fused_computation.11 | convolution fusion | flops 268435456 | bytes 18882560 | tf_op jit(solution)/shard_map/dot_general | solution.py:205
  175.9 161.6 %all-to-all-done.1.came_ref = bf16[16,44,64,128]{3,2,1,0:T(8,128)(2,1)} async-done(((bf16[16,44,64,128]{3,2,1,0:T(8,128)(2,1)}), bf16[16,44,64,128]{3,2,1,0:T(8,128)(2,1)}, u32[]{:S(2)}, u32[]{:S(2)}) %all-to-all-start.1) | async-done | bytes 11534368 | tf_op jit(solution)/shard_map/all_to_all | solution.py:194
  337.5 49.2 %all-to-all-start.2 = ((bf16[16,12,64,128]{3,2,1,0:T(8,128)(2,1)}), bf16[16,12,64,128]{3,2,1,0:T(8,128)(2,1)}, u32[]{:S(2)}, u32[]{:S(2)}) async-start(bf16[16,12,64,128]{3,2,1,0:T(8,128)(2,1)} %shard_map.77), calls=%async_computation.2 | async-start | bytes 6291456 | tf_op jit(solution)/shard_map/all_to_all | solution.py:194
  386.7 19.2 %shard_map.81 = (bf16[128,64,1024]{2,1,0:T(8,128)(2,1)}, bf16[88,64,1024]{2,1,0:T(8,128)(2,1)}) custom-call(bf16[16,44,64,128]{3,2,1,0:T(8,128)(2,1)} %all-to-all-done.1.came_ref, bf16[1024,1024]{1,0:T(8,128)(2,1)S(1)} %copy-done.3, bf16[128,64,1024]{2,1,0:T(8,128)(2,1)} %get-tuple-element.18.refs_0_), custom_call_target="tpu_custom_call", output_to_operand_aliasing={{0}: (2, {})} | custom-call | flops 11811160064 | bytes 36700160 | tf_op jit(solution)/shard_map/pallas_call | solution.py:135
  405.8 14.0 %copy.17 = bf16[11,8,64,1024]{3,1,2,0:T(8,128)(2,1)} copy(bf16[11,8,64,1024]{3,2,1,0:T(8,128)(2,1)} %bitcast.42) | data formatting | bytes 23068672
  419.8 11.9 %fusion.3 = f32[88,128]{1,0:T(8,128)S(1)} fusion(bf16[88,65536]{1,0:T(8,128)(2,1)} %bitcast.40, bf16[128,65536]{1,0:T(8,128)(2,1)} %bitcast.37), kind=kOutput, calls=%fused_computation.12 | convolution fusion | flops 1476395008 | bytes 28356608 | tf_op jit(solution)/shard_map/dot_general | solution.py:205
  431.8 14.3 %all-to-all-done.2.came_ref = bf16[16,12,64,128]{3,2,1,0:T(8,128)(2,1)} async-done(((bf16[16,12,64,128]{3,2,1,0:T(8,128)(2,1)}), bf16[16,12,64,128]{3,2,1,0:T(8,128)(2,1)}, u32[]{:S(2)}, u32[]{:S(2)}) %all-to-all-start.2) | async-done | bytes 3145760 | tf_op jit(solution)/shard_map/all_to_all | solution.py:194
  446.1 5.5 %shard_map.82 = (bf16[128,64,1024]{2,1,0:T(8,128)(2,1)}, bf16[24,64,1024]{2,1,0:T(8,128)(2,1)S(1)}) custom-call(bf16[16,12,64,128]{3,2,1,0:T(8,128)(2,1)} %all-to-all-done.2.came_ref, bf16[1024,1024]{1,0:T(8,128)(2,1)S(1)} %copy-done.3, bf16[128,64,1024]{2,1,0:T(8,128)(2,1)} %get-tuple-element.19.refs_0_), custom_call_target="tpu_custom_call", output_to_operand_aliasing={{0}: (2, {})} | custom-call | flops 3221225472 | bytes 11534336 | tf_op jit(solution)/shard_map/pallas_call | solution.py:135
  451.6 1.7 copy.18
  453.4 8.1 %fusion.4 = f32[24,128]{1,0:T(8,128)S(1)} fusion(bf16[24,65536]{1,0:T(8,128)(2,1)S(1)} %bitcast.41, bf16[128,65536]{1,0:T(8,128)(2,1)} %bitcast.38), kind=kOutput, calls=%fused_computation.13 | convolution fusion | flops 402653184 | bytes 19935232 | tf_op jit(solution)/shard_map/dot_general | solution.py:205
  461.5 22.1 %all_to_all.25 = f32[16,8,128]{2,1,0:T(8,128)S(1)} all-to-all(f32[16,8,128]{2,1,0:T(8,128)S(1)} %maximum_bitcast_fusion), channel_id=1, replica_groups=mesh['grp'=2,'row'=8,'col'=2] {'row','col'}, dimensions={0} | all-to-all | bytes 131072 | tf_op jit(solution)/shard_map/all_to_all | solution.py:163
  483.6 9.5 %all_to_all.26 = f32[16,8,128]{2,1,0:T(8,128)S(1)} all-to-all(f32[16,8,128]{2,1,0:T(8,128)S(1)} %broadcast_in_dim.22), channel_id=1, replica_groups=mesh['grp'=2,'row'=8,'col'=2] {'row','col'}, dimensions={0} | all-to-all | bytes 131072 | tf_op jit(solution)/shard_map/all_to_all | solution.py:166
  493.1 0.6 multiply_bitcast_fusion
  (16 shorter events, 0.2 us)
Async XLA Ops:
  7.2 1.8 copy-start
  7.2 56.9 %all-gather.2.cloned.1.call-start = ((), (), s32[]{:S(2)}) async-start(), calls=%async_computation.5 | async-start | bytes 4456448 | tf_op jit(solution)/shard_map/all_gather | solution.py:178
  73.9 1.3 copy-start.2
  75.2 45.5 %all-to-all-start = ((bf16[16,8,64,128]{3,2,1,0:T(8,128)(2,1)}), bf16[16,8,64,128]{3,2,1,0:T(8,128)(2,1)}, u32[]{:S(2)}, u32[]{:S(2)}) async-start(bf16[16,8,64,128]{3,2,1,0:T(8,128)(2,1)} %copy-done.2), calls=%async_computation | async-start | bytes 4194304 | tf_op jit(solution)/shard_map/all_to_all | solution.py:194
  120.8 216.7 %all-to-all-start.1 = ((bf16[16,44,64,128]{3,2,1,0:T(8,128)(2,1)}), bf16[16,44,64,128]{3,2,1,0:T(8,128)(2,1)}, u32[]{:S(2)}, u32[]{:S(2)}) async-start(bf16[16,44,64,128]{3,2,1,0:T(8,128)(2,1)} %shard_map.78), calls=%async_computation.1 | async-start | bytes 23068672 | tf_op jit(solution)/shard_map/all_to_all | solution.py:194
  150.6 9.6 %copy-start.4 = (bf16[1024,2048]{1,0:T(8,128)(2,1)S(1)}, bf16[1024,2048]{1,0:T(8,128)(2,1)}, u32[]{:S(2)}) copy-start(bf16[1024,2048]{1,0:T(8,128)(2,1)} %all-gather.2.cloned.1.call-done) | copy-start | bytes 12582916
  175.9 210.8 %copy-start.3 = (bf16[1024,1024]{1,0:T(8,128)(2,1)S(1)}, bf16[1024,1024]{1,0:T(8,128)(2,1)}, u32[]{:S(2)}) copy-start(bf16[1024,1024]{1,0:T(8,128)(2,1)} %bitcast_multiply_fusion.weight_ref) | copy-start | bytes 6291460
  337.5 108.6 %all-to-all-start.2 = ((bf16[16,12,64,128]{3,2,1,0:T(8,128)(2,1)}), bf16[16,12,64,128]{3,2,1,0:T(8,128)(2,1)}, u32[]{:S(2)}, u32[]{:S(2)}) async-start(bf16[16,12,64,128]{3,2,1,0:T(8,128)(2,1)} %shard_map.77), calls=%async_computation.2 | async-start | bytes 6291456 | tf_op jit(solution)/shard_map/all_to_all | solution.py:194
  453.4 40.4 %copy-start.1 = (s32[1,8,8]{2,1,0:T(8,128)S(1)}, s32[1,8,8]{2,1,0:T(8,128)}, u32[]{:S(2)}) copy-start(s32[1,8,8]{2,1,0:T(8,128)} %param.9) | copy-start | bytes 772
Sparse Core Ops, SparseCore 0:
  10.8 53.2 all-gather.1
